TPU v7x, 128 devices: a whole 4x4x4 slice. The times are simulated.
128 devices in a mesh: leaf: 32 (over z, y, core), rows: 4 (over x).
Axes of the slice: x: 4, y: 4, z: 4, core: 2. Of those that a mesh axis runs over, the one named last changes fastest.
Arguments:
- sigma_top: float32 [8192, 1024], P('leaf'), may hold values from -4 to 40, as said below
- panel_top: float32 [1024, 49152], P(None, 'leaf'), may hold values from -0.125 to 0.125
- diag_top: float32 [49152, 256], P('leaf'), may hold values from -4 to 20, as said below
- panel_mid: float32 [1024, 98304], P(None, ('leaf', 'rows')), may hold values from -0.125 to 0.125
- diag_mid: float32 [98304, 256], P(('leaf', 'rows')), may hold values from -4 to 20, as said below
- pattern_mid: int32 [16, 4], replicated, may hold values from 0 to 23, as said below
- panel_low: float32 [1024, 196608], P(None, ('leaf', 'rows')), may hold values from -0.125 to 0.125
- diag_low: float32 [196608, 256], P(('leaf', 'rows')), may hold values from -4 to 20, as said below
- pattern_low: int32 [32, 4], replicated, may hold values from 0 to 23, as said below
Outputs:
- cross_top: float32 [1024, 49152], P('rows', 'leaf')
- marginal_top: float32 [49152, 256], P(('leaf', 'rows'))
- cross_mid: float32 [1024, 98304], P(None, ('leaf', 'rows'))
- marginal_mid: float32 [98304, 256], P(('leaf', 'rows'))
- cross_low: float32 [1024, 196608], P(None, ('leaf', 'rows'))
- marginal_low: float32 [196608, 256], P(('leaf', 'rows'))
Inputs may be any that keep to these rules, and one draw needn't show every extreme that they name: Each block of 1024 rows of sigma_top is symmetric. `diag_top`: each 256 x 256 block is symmetric. `diag_mid`: each block of 256 rows is symmetric. `diag_low`: each block of 256 rows is symmetric. `pattern_mid`: the 4 entries of a row are different; rows 2i and 2i + 1 together name 8 different blocks. `pattern_low`: the 4 entries of a row are different; rows 2i and 2i + 1 together name 8 different blocks.
All inputs are finite; a program needn't handle non-finite values.
Results may differ from a plain program's by a relative error of at most 0.00009.
Values sent between devices are 32-bit elements; how exact they have to be, the bound alone decides.
No kernel may reach another device: no remote copies, remote signals or barrier semaphores. Data moves between devices by JAX's collectives and lax.ppermute only.
A program may use at most 192 MiB of HBM per device.

v0:
```python
import jax
import jax.numpy as jnp
from jax import lax
from jax.experimental import pallas as pl
from jax.experimental.pallas import tpu as pltpu
from jax.sharding import PartitionSpec as P

F32 = jnp.float32
BF = jnp.bfloat16
B = 256
H = 128
S = 1024
LO = 576
PK = 136
HI = S - LO + PK
VMEM = 56 * 2**20


def shift(value, step):
    n = lax.axis_size("rows")
    return lax.ppermute(value, "rows", [(i, (i + step) % n) for i in range(n)])


def partner(value, bit):
    n = lax.axis_size("leaf")
    return lax.ppermute(value, "leaf", [(i, i ^ (1 << bit)) for i in range(n)])


def tie(*values):
    return lax.optimization_barrier(values)


def split(v):
    hi = v.astype(BF)
    return hi, (v - hi.astype(F32)).astype(BF)


def mm(a, b):
    return lax.dot_general(a, b, (((1,), (0,)), ((), ())), preferred_element_type=F32)


def mm3(ah, al, bh, bl):
    return mm(ah, bh) + mm(ah, bl) + mm(al, bh)


def chunk(i):
    return pl.ds(pl.multiple_of(i * B, B), B)


def pack(d):
    a, b, c = d[:H, :H], d[:H, H:], d[H:, H:]
    row = lax.broadcasted_iota(jnp.int32, (H, H), 0)
    col = lax.broadcasted_iota(jnp.int32, (H, H), 1)
    fold = jnp.where(col >= row, a, c)
    diag = jnp.sum(jnp.where(col == row, c, 0.0), axis=0, keepdims=True)
    low = jnp.broadcast_to(diag, (PK - H, H))
    return jnp.concatenate(
        [jnp.concatenate([b, fold], 1), jnp.concatenate([low, jnp.zeros_like(low)], 1)], 0
    )


def unpack(p):
    b, fold, diag = p[:H, :H], p[:H, H:], p[H : H + 1, :H]
    row = lax.broadcasted_iota(jnp.int32, (H, H), 0)
    col = lax.broadcasted_iota(jnp.int32, (H, H), 1)
    turned = fold.T
    a = jnp.where(col >= row, fold, turned)
    c = jnp.where(col == row, diag, jnp.where(col < row, fold, turned))
    return jnp.concatenate([jnp.concatenate([a, b], 1), jnp.concatenate([b.T, c], 1)], 0)


def call(kernel, grid, in_specs, out_specs, out_shape, scratch=(), prefetch=1):
    return pl.pallas_call(
        kernel,
        grid_spec=pltpu.PrefetchScalarGridSpec(
            num_scalar_prefetch=prefetch,
            grid=grid,
            in_specs=in_specs,
            out_specs=out_specs,
            scratch_shapes=scratch,
        ),
        out_shape=out_shape,
        compiler_params=pltpu.CompilerParams(vmem_limit_bytes=VMEM),
        cost_estimate=pl.CostEstimate(flops=1024, bytes_accessed=1024, transcendentals=0),
    )


def whole(shape):
    return pl.BlockSpec(shape, lambda g, *_: (0,) * len(shape))


def shape(*dims, dtype=F32):
    return jax.ShapeDtypeStruct(dims, dtype)


def top_entry(ids, pattern, far, slot):
    child = ids[0] // 2
    return pattern[child + far * (1 - 2 * (child % 2)), slot]


def select_top(ids, pattern, panel, diag, far):
    n = panel.shape[1] // B
    half = S // 2

    def panel_spec(other):
        def index(g, ids, pattern):
            c = ids[0] % 2
            return (1 - c if other else c), top_entry(ids, pattern, far, g) % n

        return pl.BlockSpec((half, B), index)

    def kernel(ids, pattern, p0, p1, dia, to, keep, d):
        held = top_entry(ids, pattern, far, pl.program_id(0)) // n == ids[0] % 4
        to[...] = jnp.where(held, p0[...], 0.0)
        keep[...] = jnp.where(held, p1[...], 0.0)
        d[...] = jnp.where(held, pack(dia[...]), 0.0)

    wide = pl.BlockSpec((half, B), lambda g, *_: (0, g))
    tall = pl.BlockSpec((PK, B), lambda g, *_: (g, 0))
    rows = pl.BlockSpec((B, B), lambda g, ids, pattern: (top_entry(ids, pattern, far, g) % n, 0))
    return call(
        kernel,
        (4,),
        [panel_spec(True), panel_spec(False), rows],
        [wide, wide, tall],
        [shape(half, S), shape(half, S), shape(4 * PK, B)],
        prefetch=2,
    )(ids, pattern, panel, panel, diag)


def ring_step(g):
    return jnp.where(g == 0, 2, jnp.where(g == 1, 1, jnp.where(g == 2, 3, 0)))


def low_entry(ids, pattern, g):
    return pattern[ids[0], (ids[1] + ring_step(g)) % 4]


def select_low(ids, pattern, panel, panel_other, diag, diag_other):
    n = panel.shape[1] // B

    def kernel(ids, pattern, mine, other, d_mine, d_other, plus, minus, one_lo, three_hi, own_lo, own_hi):
        g = pl.program_id(0)
        b = low_entry(ids, pattern, g)
        spot = b // n
        here = spot % 4 == ids[1]
        own = spot // 4 == ids[0] % 2
        lows = (plus.at[:LO], one_lo, minus.at[HI:], own_lo)
        highs = (minus.at[:HI], plus.at[LO:], three_hi, own_hi)
        for t in range(4):

            @pl.when(g == t)
            def _(t=t):
                low, high = lows[t], highs[t]

                def chosen(u, v):
                    return jnp.where(here, jnp.where(own, u, v), 0.0)

                low[...] = chosen(mine[:LO], other[:LO])
                high[: S - LO] = chosen(mine[LO:], other[LO:])
                high[S - LO :] = pack(chosen(d_mine[...], d_other[...]))

    cols = pl.BlockSpec((S, B), lambda g, ids, pattern: (0, low_entry(ids, pattern, g) % n))
    rows = pl.BlockSpec((B, B), lambda g, ids, pattern: (low_entry(ids, pattern, g) % n, 0))
    outs = [(LO + HI, B), (LO + HI, B), (LO, B), (HI, B), (LO, B), (HI, B)]
    return call(
        kernel,
        (4,),
        [cols, cols, rows, rows],
        [whole(o) for o in outs],
        [shape(*o) for o in outs],
        prefetch=2,
    )(ids, pattern, panel, panel_other, diag, diag_other)


def join_sigma(ids, own, own_core, far, far_core):
    def kernel(ids, own, own_core, far, far_core, hi, lo):
        side, core = ids[0] // 2 % 2, ids[0] % 2
        near_half = pl.ds(pl.multiple_of(side * 512, 512), 512)
        far_half = pl.ds(pl.multiple_of((1 - side) * 512, 512), 512)
        for ref, quad, c in ((own, far, core), (own_core, far_core, 1 - core)):
            rows = chunk(2 * side + c)
            hi[rows, :], lo[rows, :] = split(ref[...])
            hi[far_half, rows], lo[far_half, rows] = split(ref[:, far_half].T)
            rows = chunk(2 * (1 - side) + c)
            hi[rows, far_half], lo[rows, far_half] = split(quad[...])

    return call(
        kernel,
        (1,),
        [whole((B, S)), whole((B, S)), whole((B, 512)), whole((B, 512))],
        [whole((S, S))] * 2,
        [shape(S, S, dtype=BF)] * 2,
    )(ids, own, own_core, far, far_core)


def top_level(ids, hi, lo, panel, diag):
    n = panel.shape[1] // B

    def kernel(ids, hi, lo, panel, diag, cross, marg):
        g = pl.program_id(0)
        x = ids[1]
        first = x // 2 * 3 + x % 2
        uh, ul = split(panel[...])
        mine = chunk(x)
        cross[...] = -mm3(hi[mine, :], lo[mine, :], uh, ul)

        @pl.when((g == first) | (g == first + 1))
        def _():
            yh, yl = split(mm3(hi[...], lo[...], uh, ul))
            th, tl = split(panel[...].T)
            term = diag[...] + mm3(th, tl, yh, yl)

            @pl.when((x % 2 == 0) & (g == first))
            def _():
                marg[:B] = term

            @pl.when((x % 2 == 0) & (g != first))
            def _():
                marg[B:] = term[:H]

            @pl.when((x % 2 == 1) & (g == first))
            def _():
                marg[:H] = term[H:]

            @pl.when((x % 2 == 1) & (g != first))
            def _():
                marg[H:] = term

    return call(
        kernel,
        (n,),
        [
            whole((S, S)),
            whole((S, S)),
            pl.BlockSpec((S, B), lambda g, *_: (0, g)),
            pl.BlockSpec((B, B), lambda g, *_: (g, 0)),
        ],
        [pl.BlockSpec((B, B), lambda g, *_: (0, g)), whole((B + H, B))],
        [shape(B, n * B), shape(B + H, B)],
    )(ids, hi, lo, panel, diag)


def form_cov(hi, lo, uh, ul, th, tl, ph, pl_, jh, jl, place_slot, diag_of):
    for d in range(4):
        place_slot(d)

    @pl.loop(0, 4)
    def _(n):
        at = chunk(n)
        ph[:, at], pl_[:, at] = split(mm3(th[...], tl[...], hi[:, at], lo[:, at]))

    for n in range(4):
        at = slice(n * B, (n + 1) * B)
        above = n * B
        value = mm3(ph[: above + B], pl_[: above + B], uh[:, at], ul[:, at])
        jh[at, at], jl[at, at] = split(value[above:] + diag_of(n))
        if n:
            jh[:above, at], jl[:above, at] = split(value[:above])
            jh[at, :above], jl[at, :above] = split(value[:above].T)


def level_step(jh, jl, panel, diag, cross, marg):
    uh, ul = split(panel[...])
    value = -mm3(jh[...], jl[...], uh, ul)
    cross[...] = value
    xh, xl = split(value)
    th, tl = split(panel[...].T)
    for a in range(panel.shape[1] // B):
        at = slice(a * B, (a + 1) * B)
        both = mm(jnp.concatenate([th[at], tl[at]], 0), xh[:, at])
        marg[at] = diag[at] - (both[:B] + both[B:] + mm(th[at], xl[:, at]))


def level_specs(n, wide):
    cols = pl.BlockSpec((S, wide * B), lambda g, *_: (0, g))
    rows = pl.BlockSpec((wide * B, B), lambda g, *_: (g, 0))
    return [cols, rows], [cols, rows], [shape(S, n * B), shape(n * B, B)]


def mid_level(ids, hi, lo, part, part_core, d_own, d_core, panel, diag):
    n = panel.shape[1] // B

    def kernel(ids, hi, lo, own, core, d0, d1, panel, diag, cross, marg, jh, jl, uh, ul, th, tl, ph, pq):
        c = ids[0] % 2

        def place_slot(d):
            at = slice(d * B, (d + 1) * B)
            for ref, which in ((own, c), (core, 1 - c)):
                rows = pl.ds(pl.multiple_of(which * 512, 512), 512)
                v = ref[:, at]
                uh[rows, at], ul[rows, at] = split(v)
                th[at, rows], tl[at, rows] = split(v.T)

        def diag_of(s):
            rows = slice(s * PK, (s + 1) * PK)
            return unpack(d0[rows] + d1[rows])

        @pl.when(pl.program_id(0) == 0)
        def _():
            form_cov(hi, lo, uh, ul, th, tl, ph, pq, jh, jl, place_slot, diag_of)

        level_step(jh, jl, panel, diag, cross, marg)

    ins, outs, shapes = level_specs(n, 1)
    return call(
        kernel,
        (n,),
        [whole((S, S))] * 2
        + [whole(part.shape)] * 2
        + [whole((4 * PK, B))] * 2
        + ins,
        outs + [whole((S, S))] * 2,
        shapes + [shape(S, S, dtype=BF)] * 2,
        [pltpu.VMEM((S, S), BF)] * 6,
    )(ids, hi, lo, part, part_core, d_own, d_core, panel, diag)


def low_level(ids, hi, lo, parts, panel, diag):
    n = panel.shape[1] // B

    def kernel(ids, hi, lo, *refs):
        own_lo, own_hi, left_lo, right_hi, from_left, from_right = refs[:6]
        panel, diag, cross, marg = refs[6:10]
        uh, ul, th, tl, ph, pq, jh, jl, dd = refs[10:]
        x = ids[1]
        lows = (own_lo, from_right.at[:LO], from_left.at[HI:], left_lo)
        highs = (own_hi, right_hi, from_right.at[LO:], from_left.at[:HI])

        def place_slot(d):
            slot = (x + d) % 4
            at = chunk(slot)
            v = jnp.concatenate([lows[d][...], highs[d][: S - LO]], 0)
            uh[:, at], ul[:, at] = split(v)
            th[at, :], tl[at, :] = split(v.T)
            dd[slot] = highs[d][S - LO :]

        @pl.when(pl.program_id(0) == 0)
        def _():
            form_cov(hi, lo, uh, ul, th, tl, ph, pq, jh, jl, place_slot, lambda s: unpack(dd[s]))

        level_step(jh, jl, panel, diag, cross, marg)

    ins, outs, shapes = level_specs(n, 2)
    return call(
        kernel,
        (n // 2,),
        [whole((S, S))] * 2 + [whole(p.shape) for p in parts] + ins,
        outs,
        shapes,
        [pltpu.VMEM((S, S), BF)] * 8 + [pltpu.VMEM((4, PK, B), F32)],
    )(ids, hi, lo, *parts, panel, diag)


def local(
    sigma_top, panel_top, diag_top, panel_mid, diag_mid, pattern_mid, panel_low, diag_low, pattern_low
):
    leaf = lax.axis_index("leaf")
    x = lax.axis_index("rows")
    ids = jnp.stack([leaf, x]).astype(jnp.int32)
    side = leaf // 2 % 2
    half = S // 2

    panel_other, diag_other = partner((panel_mid, diag_mid), 0)
    quad = jnp.where(side == 0, sigma_top[:, :half], sigma_top[:, half:])
    quad_far = partner(quad, 1)
    to_far, keep_far, d_far = select_top(ids, pattern_mid, panel_top, diag_top, 1)
    core_far = partner(to_far, 0)

    plus, minus, one_lo, three_hi, own_lo, own_hi = select_low(
        ids, pattern_low, panel_mid, panel_other, diag_mid, diag_other
    )
    plus, minus, quad_far, sigma_ = tie(plus, minus, quad_far, sigma_top)
    r_plus = shift(plus, 1)
    r_minus = shift(minus, -1)
    sig_core = partner(sigma_, 0)
    quad_core = partner(quad_far, 0)

    far_sum, sig_core = tie(keep_far + core_far, sig_core)
    recv = partner(far_sum, 1)
    hi, lo = join_sigma(ids, sigma_top, sig_core, quad_far, quad_core)
    cross_top, marginal_top = top_level(ids, hi, lo, panel_top, diag_top)
    r_plus, r_minus, cross_top, panel_top_, d_far = tie(r_plus, r_minus, cross_top, panel_top, d_far)
    to_own, keep_own, d_keep = select_top(ids, pattern_mid, panel_top_, diag_top, 0)
    core_own = partner(to_own, 0)
    d_recv = partner(d_far, 1)
    r_one_lo = shift(one_lo + r_plus[:LO], 1)
    r_three_hi = shift(three_hi + r_minus[:HI], -1)
    own_lo = own_lo + r_minus[HI:]
    own_hi = own_hi + r_plus[LO:]

    own_lo = own_lo + r_one_lo
    own_hi = own_hi + r_three_hi
    own_lo, own_hi, keep_own = tie(own_lo, own_hi, keep_own)
    left_lo, right_hi = shift(own_lo, 1), shift(own_hi, -1)

    left_lo, right_hi, recv, d_recv = tie(left_lo, right_hi, recv, d_recv)
    part = keep_own + core_own + recv
    part_core = partner(part, 0)
    d_part = d_keep + d_recv
    d_core = partner(d_part, 0)

    next_plus = jnp.concatenate([own_hi, left_lo], 0)
    next_minus = jnp.concatenate([own_lo, right_hi], 0)
    next_plus, next_minus, hi = tie(next_plus, next_minus, hi)
    from_left = shift(next_plus, 1)
    from_right = shift(next_minus, -1)
    cross_mid, marginal_mid, mid_hi, mid_lo = mid_level(
        ids, hi, lo, part, part_core, d_part, d_core, panel_mid, diag_mid
    )
    cross_low, marginal_low = low_level(
        ids,
        mid_hi,
        mid_lo,
        [own_lo, own_hi, left_lo, right_hi, from_left, from_right],
        panel_low,
        diag_low,
    )
    return (cross_top, marginal_top, cross_mid, marginal_mid, cross_low, marginal_low)


def solution(mesh):
    return jax.shard_map(
        local,
        mesh=mesh,
        in_specs=(
            P("leaf", None),
            P(None, "leaf"),
            P("leaf", None),
            P(None, ("leaf", "rows")),
            P(("leaf", "rows"), None),
            P(),
            P(None, ("leaf", "rows")),
            P(("leaf", "rows"), None),
            P(),
        ),
        out_specs=(
            P("rows", "leaf"),
            P(("leaf", "rows"), None),
            P(None, ("leaf", "rows")),
            P(("leaf", "rows"), None),
            P(None, ("leaf", "rows")),
            P(("leaf", "rows"), None),
        ),
        check_vma=False,
    )
```

profile of v0, /device:TPU:1, one launch (start us, length us, event | category | flops | bytes accessed | tf_op | source)
XLA Modules:
  0.0 167.9 jit_solution(7198739730403666718)
XLA Ops:
  0.6 1.5 collective-permute-start
  2.1 1.3 copy.16.pattern
  4.1 6.3 %shard_map.137 = (f32[512,1024]{1,0:T(8,128)}, f32[512,1024]{1,0:T(8,128)}, f32[544,256]{1,0:T(8,128)}) custom-call(s32[2]{0:T(128)} %pad_add_fusion.ids, s32[16,4]{1,0:T(8,128)} %copy.16.pattern, f32[1024,1536]{1,0:T(8,128)} %p1.2, f32[1024,1536]{1,0:T(8,128)} %p1.2, f32[1536,256]{1,0:T(8,128)} %dia.3), custom_call_target="tpu_custom_call" | custom-call | flops 1024 | bytes 1024 | tf_op jit(solution)/shard_map/pallas_call | solution.py:121
  11.0 1.4 collective-permute-start.2
  13.1 2.3 %collective-permute-done.1.d_other = f32[768,256]{1,0:T(8,128)S(1)} collective-permute-done((f32[768,256]{1,0:T(8,128)S(1)}, f32[768,256]{1,0:T(8,128)S(1)}, u32[]{:S(2)}, u32[]{:S(2)}) %collective-permute-start.1) | collective-permute-done | bytes 786464 | tf_op jit(solution)/shard_map/ppermute | solution.py:26
  15.3 0.9 copy-done.14
  16.2 7.4 %shard_map.136 = (f32[1160,256]{1,0:T(8,128)}, f32[1160,256]{1,0:T(8,128)}, f32[576,256]{1,0:T(8,128)}, f32[584,256]{1,0:T(8,128)}, f32[576,256]{1,0:T(8,128)}, /*index=5*/f32[584,256]{1,0:T(8,128)}) custom-call(s32[2]{0:T(128)} %pad_add_fusion.ids, s32[32,4]{1,0:T(8,128)} %copy.15.pattern, f32[1024,768]{1,0:T(8,128)} %panel.3, ...), custom_call_target="tpu_custom_call" | custom-call | flops 1024 | bytes 1024 | tf_op jit(solution)/shard_map/pallas_call | solution.py:166
  23.6 1.1 collective-permute-done.2.far
  24.7 1.3 collective-permute-start.3
  26.0 1.4 collective-permute-start.4
  27.4 1.4 collective-permute-start.6
  28.8 2.1 %add.36 = f32[512,1024]{1,0:T(8,128)S(1)} add(f32[512,1024]{1,0:T(8,128)S(1)} %copy-done.8, f32[512,1024]{1,0:T(8,128)} %collective-permute-done.5) | non-fusion elementwise | flops 524288 | bytes 6291456 | tf_op jit(solution)/shard_map/add | solution.py:379
  30.9 0.9 collective-permute-done.6.own_core
  31.8 1.3 collective-permute-start.12
  33.9 5.3 %shard_map.138 = (bf16[1024,1024]{1,0:T(8,128)(2,1)}, bf16[1024,1024]{1,0:T(8,128)(2,1)}) custom-call(s32[2]{0:T(128)} %pad_add_fusion.ids, f32[256,1024]{1,0:T(8,128)} %own.1, f32[256,1024]{1,0:T(8,128)} %copy-done.13, f32[256,512]{1,0:T(8,128)} %collective-permute-done.2.far, f32[256,512]{1,0:T(8,128)} %copy-done.21), custom_call_target="tpu_custom_call" | custom-call | flops 1024 | bytes 1024 | tf_op jit(solution)/shard_map/pallas_call | solution.py:188
  39.2 15.2 %shard_map.139 = (f32[256,1536]{1,0:T(8,128)}, f32[384,256]{1,0:T(8,128)}) custom-call(s32[2]{0:T(128)} %pad_add_fusion.ids, bf16[1024,1024]{1,0:T(8,128)(2,1)} %get-tuple-element.78.hi, bf16[1024,1024]{1,0:T(8,128)(2,1)} %get-tuple-element.59.lo, f32[1024,1536]{1,0:T(8,128)} %p1.2, f32[1536,256]{1,0:T(8,128)} %dia.3), custom_call_target="tpu_custom_call" | custom-call | flops 1024 | bytes 1024 | tf_op jit(solution)/shard_map/pallas_call | solution.py:230
  54.4 6.2 %shard_map.140 = (f32[512,1024]{1,0:T(8,128)}, f32[512,1024]{1,0:T(8,128)}, f32[544,256]{1,0:T(8,128)}) custom-call(s32[2]{0:T(128)} %pad_add_fusion.ids, s32[16,4]{1,0:T(8,128)} %copy.16.pattern, f32[1024,1536]{1,0:T(8,128)} %p1.2, f32[1024,1536]{1,0:T(8,128)} %p1.2, f32[1536,256]{1,0:T(8,128)} %dia.3), custom_call_target="tpu_custom_call" | custom-call | flops 1024 | bytes 1024 | tf_op jit(solution)/shard_map/pallas_call | solution.py:121
  61.4 0.9 collective-permute-start.8
  62.5 1.9 %collective-permute-start.9 = (f32[584,256]{1,0:T(8,128)S(1)}, f32[584,256]{1,0:T(8,128)S(1)}, u32[]{:S(2)}, u32[]{:S(2)}) collective-permute-start(f32[584,256]{1,0:T(8,128)S(1)} %slice_add_fusion), channel_id=1, source_target_pairs={{0,3},{1,0},{2,1},{3,2},{4,7},{5,4},{6,5},{7,6},{8,11},{9,8},{10,9... | collective-permute-start | bytes 1794056 | tf_op jit(solution)/shard_map/ppermute | solution.py:21
  64.4 13.3 %collective-permute-done.8 = f32[576,256]{1,0:T(8,128)S(1)} collective-permute-done((f32[576,256]{1,0:T(8,128)S(1)}, f32[576,256]{1,0:T(8,128)S(1)}, u32[]{:S(2)}, u32[]{:S(2)}) %collective-permute-start.8) | collective-permute-done | bytes 589856 | tf_op jit(solution)/shard_map/ppermute | solution.py:21
  78.0 2.5 %collective-permute-start.11 = (f32[584,256]{1,0:T(8,128)S(1)}, f32[584,256]{1,0:T(8,128)S(1)}, u32[]{:S(2)}, u32[]{:S(2)}) collective-permute-start(f32[584,256]{1,0:T(8,128)S(1)} %add_add_fusion.1.refs_1_), channel_id=1, source_target_pairs={{0,3},{1,0},{2,1},{3,2},{4,7},{5,4},{6,5},{7,6},{8,11},{9,8},{10,9... | collective-permute-start | bytes 1794056 | tf_op jit(solution)/shard_map/ppermute | solution.py:21
  81.0 12.2 %collective-permute-done.13 = f32[544,256]{1,0:T(8,128)S(1)} collective-permute-done((f32[544,256]{1,0:T(8,128)S(1)}, f32[544,256]{1,0:T(8,128)S(1)}, u32[]{:S(2)}, u32[]{:S(2)}) %collective-permute-start.13) | collective-permute-done | bytes 557088 | tf_op jit(solution)/shard_map/ppermute | solution.py:26
  93.1 1.9 %collective-permute-done.10.refs_2_ = f32[576,256]{1,0:T(8,128)S(1)} collective-permute-done((f32[576,256]{1,0:T(8,128)S(1)}, f32[576,256]{1,0:T(8,128)S(1)}, u32[]{:S(2)}, u32[]{:S(2)}) %collective-permute-start.10) | collective-permute-done | bytes 589856 | tf_op jit(solution)/shard_map/ppermute | solution.py:21
  95.8 2.5 %collective-permute-start.15 = (f32[512,1024]{1,0:T(8,128)S(1)}, f32[512,1024]{1,0:T(8,128)S(1)}, u32[]{:S(2)}, u32[]{:S(2)}) collective-permute-start(f32[512,1024]{1,0:T(8,128)S(1)} %add_add_fusion.own), channel_id=1, source_target_pairs={{0,4},{4,0},{8,12},{12,8},{16,20},{20,16},{24,28},{28,24},{32,36},... | collective-permute-start | bytes 6291464 | tf_op jit(solution)/shard_map/ppermute | solution.py:26
  98.8 2.7 %collective-permute-start.18 = (f32[1160,256]{1,0:T(8,128)S(1)}, f32[1160,256]{1,0:T(8,128)S(1)}, u32[]{:S(2)}, u32[]{:S(2)}) collective-permute-start(f32[1160,256]{1,0:T(8,128)S(1)} %get-tuple-element.89), channel_id=1, source_target_pairs={{0,3},{1,0},{2,1},{3,2},{4,7},{5,4},{6,5},{7,6},{8,11},{9,8},{10,9... | collective-permute-start | bytes 3563528 | tf_op jit(solution)/shard_map/ppermute | solution.py:21
  101.5 1.4 collective-permute-start.16
  103.0 1.6 collective-permute-done.16.d1
  104.6 0.8 copy-done.20
  105.4 1.3 copy-done.10
  106.7 27.5 %shard_map.141 = (f32[1024,768]{1,0:T(8,128)}, f32[768,256]{1,0:T(8,128)}, bf16[1024,1024]{1,0:T(8,128)(2,1)}, bf16[1024,1024]{1,0:T(8,128)(2,1)}) custom-call(s32[2]{0:T(128)} %pad_add_fusion.ids, bf16[1024,1024]{1,0:T(8,128)(2,1)} %get-tuple-element.78.hi, bf16[1024,1024]{1,0:T(8,128)(2,1)} %get-tuple-element.59.lo, f32[512,1024]{1,0:T(8,128)} %copy-done, ...), custom_call_target="tpu_custom_call" | custom-call | flops 1024 | bytes 1024 | tf_op jit(solution)/shard_map/pallas_call | solution.py:306
  134.2 1.0 copy-done.11
  135.6 32.3 %shard_map.142 = (f32[1024,1536]{1,0:T(8,128)}, f32[1536,256]{1,0:T(8,128)}) custom-call(s32[2]{0:T(128)} %pad_add_fusion.ids, bf16[1024,1024]{1,0:T(8,128)(2,1)} %get-tuple-element.86.hi, bf16[1024,1024]{1,0:T(8,128)(2,1)} %get-tuple-element.87.lo, f32[576,256]{1,0:T(8,128)} %copy-done.2, f32[584,256]{1,0:T(8,128)} %copy-done.1, f32[576,256]{1,0:T(8,128)} %copy-done.6, ...), custom_call_target="tpu_custom_call" | custom-call | flops 1024 | bytes 1024 | tf_op jit(solution)/shard_map/pallas_call | solution.py:345
  (73 shorter events, 6.2 us)
Async XLA Ops:
  0.6 14.7 %collective-permute-start = (f32[1024,768]{1,0:T(8,128)}, f32[1024,768]{1,0:T(8,128)}, u32[]{:S(2)}, u32[]{:S(2)}) collective-permute-start(f32[1024,768]{1,0:T(8,128)} %panel.3), channel_id=1, source_target_pairs={{0,4},{4,0},{8,12},{12,8},{16,20},{20,16},{24,28},{28,24},{32,36},... | collective-permute-start | bytes 9437192 | tf_op jit(solution)/shard_map/ppermute | solution.py:26
  4.1 6.3 %copy-start.4 = (f32[768,256]{1,0:T(8,128)S(1)}, f32[768,256]{1,0:T(8,128)}, u32[]{:S(2)}) copy-start(f32[768,256]{1,0:T(8,128)} %diag.3) | copy-start | bytes 2359300
  4.1 6.8 %copy-start.3 = (f32[256,1024]{1,0:T(8,128)S(1)}, f32[256,1024]{1,0:T(8,128)}, u32[]{:S(2)}) copy-start(f32[256,1024]{1,0:T(8,128)} %own.1) | copy-start | bytes 3145732
  4.1 8.2 %copy-start.22 = (s32[32,4]{0,1:T(4,128)S(1)}, s32[32,4]{0,1:T(4,128)}, u32[]{:S(2)}) copy-start(s32[32,4]{0,1:T(4,128)} %param.17) | copy-start | bytes 1540
  10.4 18.4 %collective-permute-start.5 = (f32[512,1024]{1,0:T(8,128)}, f32[512,1024]{1,0:T(8,128)}, u32[]{:S(2)}, u32[]{:S(2)}) collective-permute-start(f32[512,1024]{1,0:T(8,128)} %get-tuple-element.54), channel_id=1, source_target_pairs={{0,4},{4,0},{8,12},{12,8},{16,20},{20,16},{24,28},{28,24},{32,36},... | collective-permute-start | bytes 6291464 | tf_op jit(solution)/shard_map/ppermute | solution.py:26
  10.4 4.9 %collective-permute-start.1 = (f32[768,256]{1,0:T(8,128)S(1)}, f32[768,256]{1,0:T(8,128)S(1)}, u32[]{:S(2)}, u32[]{:S(2)}) collective-permute-start(f32[768,256]{1,0:T(8,128)S(1)} %copy-done.4), channel_id=1, source_target_pairs={{0,4},{4,0},{8,12},{12,8},{16,20},{20,16},{24,28},{28,24},{32,36},... | collective-permute-start | bytes 2359304 | tf_op jit(solution)/shard_map/ppermute | solution.py:26
  11.0 13.7 %collective-permute-start.2 = (f32[256,512]{1,0:T(8,128)S(1)}, f32[256,512]{1,0:T(8,128)}, u32[]{:S(2)}, u32[]{:S(2)}) collective-permute-start(f32[256,512]{1,0:T(8,128)S(1)} %slice_select_fusion), channel_id=1, source_target_pairs={{0,8},{4,12},{8,0},{12,4},{16,24},{20,28},{24,16},{28,20},{32,40},... | collective-permute-start | bytes 1572872 | tf_op jit(solution)/shard_map/ppermute | solution.py:26
  13.1 15.7 %copy-start.8 = (f32[512,1024]{1,0:T(8,128)S(1)}, f32[512,1024]{1,0:T(8,128)}, u32[]{:S(2)}) copy-start(f32[512,1024]{1,0:T(8,128)} %get-tuple-element.53) | copy-start | bytes 6291460
  24.7 29.7 %collective-permute-start.3 = (f32[1160,256]{1,0:T(8,128)}, f32[1160,256]{1,0:T(8,128)S(1)}, u32[]{:S(2)}, u32[]{:S(2)}) collective-permute-start(f32[1160,256]{1,0:T(8,128)} %get-tuple-element.51), channel_id=1, source_target_pairs={{0,1},{1,2},{2,3},{3,0},{4,5},{5,6},{6,7},{7,4},{8,9},{9,10},{10,1... | collective-permute-start | bytes 3563528 | tf_op jit(solution)/shard_map/ppermute | solution.py:21
  26.0 28.5 %collective-permute-start.4 = (f32[1160,256]{1,0:T(8,128)}, f32[1160,256]{1,0:T(8,128)S(1)}, u32[]{:S(2)}, u32[]{:S(2)}) collective-permute-start(f32[1160,256]{1,0:T(8,128)} %get-tuple-element.52), channel_id=1, source_target_pairs={{0,3},{1,0},{2,1},{3,2},{4,7},{5,4},{6,5},{7,6},{8,11},{9,8},{10,9... | collective-permute-start | bytes 3563528 | tf_op jit(solution)/shard_map/ppermute | solution.py:21
  27.4 4.5 %collective-permute-start.6 = (f32[256,1024]{1,0:T(8,128)S(1)}, f32[256,1024]{1,0:T(8,128)S(1)}, u32[]{:S(2)}, u32[]{:S(2)}) collective-permute-start(f32[256,1024]{1,0:T(8,128)S(1)} %copy-done.3), channel_id=1, source_target_pairs={{0,4},{4,0},{8,12},{12,8},{16,20},{20,16},{24,28},{28,24},{32,36},... | collective-permute-start | bytes 3145736 | tf_op jit(solution)/shard_map/ppermute | solution.py:26
  28.8 4.3 %collective-permute-start.7 = (f32[256,512]{1,0:T(8,128)}, f32[256,512]{1,0:T(8,128)S(1)}, u32[]{:S(2)}, u32[]{:S(2)}) collective-permute-start(f32[256,512]{1,0:T(8,128)} %collective-permute-done.2.far), channel_id=1, source_target_pairs={{0,4},{4,0},{8,12},{12,8},{16,20},{20,16},{24,28},{28,24},{32,36},... | collective-permute-start | bytes 1572872 | tf_op jit(solution)/shard_map/ppermute | solution.py:26
  31.8 63.2 %collective-permute-start.12 = (f32[512,1024]{1,0:T(8,128)S(1)}, f32[512,1024]{1,0:T(8,128)S(1)}, u32[]{:S(2)}, u32[]{:S(2)}) collective-permute-start(f32[512,1024]{1,0:T(8,128)S(1)} %add.36), channel_id=1, source_target_pairs={{0,8},{4,12},{8,0},{12,4},{16,24},{20,28},{24,16},{28,20},{32,40},... | collective-permute-start | bytes 6291464 | tf_op jit(solution)/shard_map/ppermute | solution.py:26
  54.4 6.9 %copy-start.17 = (f32[576,256]{1,0:T(8,128)S(1)}, f32[576,256]{1,0:T(8,128)}, u32[]{:S(2)}) copy-start(f32[576,256]{1,0:T(8,128)} %get-tuple-element.66) | copy-start | bytes 1769476
  60.6 17.0 %copy-start.18 = (f32[576,256]{1,0:T(8,128)S(1)}, f32[576,256]{1,0:T(8,128)}, u32[]{:S(2)}) copy-start(f32[576,256]{1,0:T(8,128)} %get-tuple-element.64) | copy-start | bytes 1769476
  60.6 34.5 %collective-permute-start.14 = (f32[512,1024]{1,0:T(8,128)}, f32[512,1024]{1,0:T(8,128)S(1)}, u32[]{:S(2)}, u32[]{:S(2)}) collective-permute-start(f32[512,1024]{1,0:T(8,128)} %get-tuple-element.80), channel_id=1, source_target_pairs={{0,4},{4,0},{8,12},{12,8},{16,20},{20,16},{24,28},{28,24},{32,36},... | collective-permute-start | bytes 6291464 | tf_op jit(solution)/shard_map/ppermute | solution.py:26
  61.4 16.4 %copy-start.16 = (f32[584,256]{1,0:T(8,128)S(1)}, f32[584,256]{1,0:T(8,128)}, u32[]{:S(2)}) copy-start(f32[584,256]{1,0:T(8,128)} %get-tuple-element.68) | copy-start | bytes 1794052
  61.4 16.2 %collective-permute-start.8 = (f32[576,256]{1,0:T(8,128)S(1)}, f32[576,256]{1,0:T(8,128)S(1)}, u32[]{:S(2)}, u32[]{:S(2)}) collective-permute-start(f32[576,256]{1,0:T(8,128)S(1)} %slice_add_fusion.1), channel_id=1, source_target_pairs={{0,1},{1,2},{2,3},{3,0},{4,5},{5,6},{6,7},{7,4},{8,9},{9,10},{10,1... | collective-permute-start | bytes 1769480 | tf_op jit(solution)/shard_map/ppermute | solution.py:21
  62.5 15.4 %collective-permute-start.9 = (f32[584,256]{1,0:T(8,128)S(1)}, f32[584,256]{1,0:T(8,128)S(1)}, u32[]{:S(2)}, u32[]{:S(2)}) collective-permute-start(f32[584,256]{1,0:T(8,128)S(1)} %slice_add_fusion), channel_id=1, source_target_pairs={{0,3},{1,0},{2,1},{3,2},{4,7},{5,4},{6,5},{7,6},{8,11},{9,8},{10,9... | collective-permute-start | bytes 1794056 | tf_op jit(solution)/shard_map/ppermute | solution.py:21
  77.6 17.4 %copy-start.9 = (f32[512,1024]{1,0:T(8,128)S(1)}, f32[512,1024]{1,0:T(8,128)}, u32[]{:S(2)}) copy-start(f32[512,1024]{1,0:T(8,128)} %get-tuple-element.79) | copy-start | bytes 6291460
  77.8 20.4 %copy-start.2 = (f32[576,256]{1,0:T(8,128)}, f32[576,256]{1,0:T(8,128)S(1)}, u32[]{:S(2)}) copy-start(f32[576,256]{1,0:T(8,128)S(1)} %add_add_fusion.2.refs_0_) | copy-start | bytes 1769476
  78.0 20.3 %copy-start.1 = (f32[584,256]{1,0:T(8,128)}, f32[584,256]{1,0:T(8,128)S(1)}, u32[]{:S(2)}) copy-start(f32[584,256]{1,0:T(8,128)S(1)} %add_add_fusion.1.refs_1_) | copy-start | bytes 1794052
  78.0 17.0 %collective-permute-start.11 = (f32[584,256]{1,0:T(8,128)S(1)}, f32[584,256]{1,0:T(8,128)S(1)}, u32[]{:S(2)}, u32[]{:S(2)}) collective-permute-start(f32[584,256]{1,0:T(8,128)S(1)} %add_add_fusion.1.refs_1_), channel_id=1, source_target_pairs={{0,3},{1,0},{2,1},{3,2},{4,7},{5,4},{6,5},{7,6},{8,11},{9,8},{10,9... | collective-permute-start | bytes 1794056 | tf_op jit(solution)/shard_map/ppermute | solution.py:21
  80.5 14.6 %collective-permute-start.10 = (f32[576,256]{1,0:T(8,128)S(1)}, f32[576,256]{1,0:T(8,128)S(1)}, u32[]{:S(2)}, u32[]{:S(2)}) collective-permute-start(f32[576,256]{1,0:T(8,128)S(1)} %add_add_fusion.2.refs_0_), channel_id=1, source_target_pairs={{0,1},{1,2},{2,3},{3,0},{4,5},{5,6},{6,7},{7,4},{8,9},{9,10},{10,1... | collective-permute-start | bytes 1769480 | tf_op jit(solution)/shard_map/ppermute | solution.py:21
  80.5 12.6 %collective-permute-start.13 = (f32[544,256]{1,0:T(8,128)S(1)}, f32[544,256]{1,0:T(8,128)S(1)}, u32[]{:S(2)}, u32[]{:S(2)}) collective-permute-start(f32[544,256]{1,0:T(8,128)S(1)} %copy-done.23), channel_id=1, source_target_pairs={{0,8},{4,12},{8,0},{12,4},{16,24},{20,28},{24,16},{28,20},{32,40},... | collective-permute-start | bytes 1671176 | tf_op jit(solution)/shard_map/ppermute | solution.py:26
  95.0 3.2 %copy-start.6 = (f32[576,256]{1,0:T(8,128)}, f32[576,256]{1,0:T(8,128)S(1)}, u32[]{:S(2)}) copy-start(f32[576,256]{1,0:T(8,128)S(1)} %collective-permute-done.10.refs_2_) | copy-start | bytes 1769476
  95.0 3.2 %copy-start.5 = (f32[584,256]{1,0:T(8,128)}, f32[584,256]{1,0:T(8,128)S(1)}, u32[]{:S(2)}) copy-start(f32[584,256]{1,0:T(8,128)S(1)} %collective-permute-done.11.refs_3_) | copy-start | bytes 1794052
  95.8 5.7 %copy-start.19 = (f32[544,256]{1,0:T(8,128)S(1)}, f32[544,256]{1,0:T(8,128)}, u32[]{:S(2)}) copy-start(f32[544,256]{1,0:T(8,128)} %get-tuple-element.82) | copy-start | bytes 1671172
  95.8 8.8 %collective-permute-start.15 = (f32[512,1024]{1,0:T(8,128)S(1)}, f32[512,1024]{1,0:T(8,128)S(1)}, u32[]{:S(2)}, u32[]{:S(2)}) collective-permute-start(f32[512,1024]{1,0:T(8,128)S(1)} %add_add_fusion.own), channel_id=1, source_target_pairs={{0,4},{4,0},{8,12},{12,8},{16,20},{20,16},{24,28},{28,24},{32,36},... | collective-permute-start | bytes 6291464 | tf_op jit(solution)/shard_map/ppermute | solution.py:26
  98.5 35.6 %collective-permute-start.17 = (f32[1160,256]{1,0:T(8,128)S(1)}, f32[1160,256]{1,0:T(8,128)S(1)}, u32[]{:S(2)}, u32[]{:S(2)}) collective-permute-start(f32[1160,256]{1,0:T(8,128)S(1)} %get-tuple-element.88), channel_id=1, source_target_pairs={{0,1},{1,2},{2,3},{3,0},{4,5},{5,6},{6,7},{7,4},{8,9},{9,10},{10,1... | collective-permute-start | bytes 3563528 | tf_op jit(solution)/shard_map/ppermute | solution.py:21
  98.8 35.4 %collective-permute-start.18 = (f32[1160,256]{1,0:T(8,128)S(1)}, f32[1160,256]{1,0:T(8,128)S(1)}, u32[]{:S(2)}, u32[]{:S(2)}) collective-permute-start(f32[1160,256]{1,0:T(8,128)S(1)} %get-tuple-element.89), channel_id=1, source_target_pairs={{0,3},{1,0},{2,1},{3,2},{4,7},{5,4},{6,5},{7,6},{8,11},{9,8},{10,9... | collective-permute-start | bytes 3563528 | tf_op jit(solution)/shard_map/ppermute | solution.py:21
  101.5 3.0 %collective-permute-start.16 = (f32[544,256]{1,0:T(8,128)S(1)}, f32[544,256]{1,0:T(8,128)S(1)}, u32[]{:S(2)}, u32[]{:S(2)}) collective-permute-start(f32[544,256]{1,0:T(8,128)S(1)} %add.45.d0), channel_id=1, source_target_pairs={{0,4},{4,0},{8,12},{12,8},{16,20},{20,16},{24,28},{28,24},{32,36},... | collective-permute-start | bytes 1671176 | tf_op jit(solution)/shard_map/ppermute | solution.py:26
  (11 other events, 18.0 us)
where the time goes:
time: 169 us; the launch traced here: 168 us
  Pallas kernels  100 us (59%)
  waiting for transfers between devices  33.2 us (20%)
  starting transfers between devices  22.1 us (13%)
  local copies, waits for them, and re-layouts  7.33 us (4%)
  other arithmetic  4.36 us (3%)
    pallas_call x1, Pallas kernels, low_level(): call(kernel, (n // 2,), [whole((S, S))] * 2 + [whole(p.shape) for p in pa...  32.3 us
    pallas_call x1, Pallas kernels, mid_level(): call(kernel, (n,), [whole((S, S))] * 2 + [whole(part.shape)] * 2 + [whole...  27.5 us
    ppermute x11, waiting for transfers between devices, partner(): return lax.ppermute(value, 'leaf', [(i, i ^ 1 << bit) for i in range(n)])  18 us
    pallas_call x1, Pallas kernels, top_level(): call(kernel, (n,), [whole((S, S)), whole((S, S)), pl.BlockSpec((S, B), la...  15.2 us
    ppermute x8, waiting for transfers between devices, shift(): return lax.ppermute(value, 'rows', [(i, (i + step) % n) for i in range(n)])  15.2 us
    pallas_call x2, Pallas kernels, select_top(): call(kernel, (4,), [panel_spec(True), panel_spec(False), rows], [wide, wi...  12.4 us
    ppermute x11, starting transfers between devices, partner(): return lax.ppermute(value, 'leaf', [(i, i ^ 1 << bit) for i in range(n)])  11.2 us
    ppermute x8, starting transfers between devices, shift(): return lax.ppermute(value, 'rows', [(i, (i + step) % n) for i in range(n)])  10.9 us
  transfers between devices with their start and end apart: 19, of which 7 were waited for; matrix products, arithmetic and copies ran while one was open for 3% of the time, Pallas kernels for 40%

commit v1 on v0

--- a/solution.py
+++ b/solution.py
@@ -367,6 +367,9 @@
     to_far, keep_far, d_far = select_top(ids, pattern_mid, panel_top, diag_top, 1)
     core_far = partner(to_far, 0)
 
+    to_own, keep_own, d_keep = select_top(ids, pattern_mid, panel_top, diag_top, 0)
+    panel_other, to_own = tie(panel_other, to_own)
+
     plus, minus, one_lo, three_hi, own_lo, own_hi = select_low(
         ids, pattern_low, panel_mid, panel_other, diag_mid, diag_other
     )
@@ -380,8 +383,7 @@
     recv = partner(far_sum, 1)
     hi, lo = join_sigma(ids, sigma_top, sig_core, quad_far, quad_core)
     cross_top, marginal_top = top_level(ids, hi, lo, panel_top, diag_top)
-    r_plus, r_minus, cross_top, panel_top_, d_far = tie(r_plus, r_minus, cross_top, panel_top, d_far)
-    to_own, keep_own, d_keep = select_top(ids, pattern_mid, panel_top_, diag_top, 0)
+    r_plus, r_minus, cross_top, to_own, d_far = tie(r_plus, r_minus, cross_top, to_own, d_far)
     core_own = partner(to_own, 0)
     d_recv = partner(d_far, 1)
     r_one_lo = shift(one_lo + r_plus[:LO], 1)

time: 169 us -> 166 us (0.982)
  starting transfers between devices: 22.1 us -> 19.6 us
    ppermute x11, starting transfers between devices: 11.2 us -> 8.5 us  [partner(): return lax.ppermute(value, 'leaf', [(i, i ^ 1 << bit) for i in range(n)])]
  transfers between devices with their start and end apart: 19 -> 19, of which waited for: 7 -> 5; matrix products, arithmetic and copies ran while one was open for 3% -> 3% of each run, Pallas kernels for 40% -> 41%
where the time goes in v1:
time: 166 us; the launch traced here: 165 us
  Pallas kernels  101 us (61%)
  waiting for transfers between devices  31.7 us (19%)
  starting transfers between devices  19.6 us (12%)
  local copies, waits for them, and re-layouts  7.81 us (5%)
  other arithmetic  4.36 us (3%)
    pallas_call x1, Pallas kernels, low_level(): call(kernel, (n // 2,), [whole((S, S))] * 2 + [whole(p.shape) for p in pa...  32.3 us
    pallas_call x1, Pallas kernels, mid_level(): call(kernel, (n,), [whole((S, S))] * 2 + [whole(part.shape)] * 2 + [whole...  27.5 us
    ppermute x11, waiting for transfers between devices, partner(): return lax.ppermute(value, 'leaf', [(i, i ^ 1 << bit) for i in range(n)])  18.1 us
    pallas_call x1, Pallas kernels, top_level(): call(kernel, (n,), [whole((S, S)), whole((S, S)), pl.BlockSpec((S, B), la...  15.4 us
    ppermute x8, waiting for transfers between devices, shift(): return lax.ppermute(value, 'rows', [(i, (i + step) % n) for i in range(n)])  13.6 us
    pallas_call x2, Pallas kernels, select_top(): call(kernel, (4,), [panel_spec(True), panel_spec(False), rows], [wide, wi...  12.3 us
    ppermute x8, starting transfers between devices, shift(): return lax.ppermute(value, 'rows', [(i, (i + step) % n) for i in range(n)])  11.1 us
    ppermute x11, starting transfers between devices, partner(): return lax.ppermute(value, 'leaf', [(i, i ^ 1 << bit) for i in range(n)])  8.5 us
  transfers between devices with their start and end apart: 19, of which 5 were waited for; matrix products, arithmetic and copies ran while one was open for 3% of the time, Pallas kernels for 41%

profile of v1, /device:TPU:1, one launch (start us, length us, event | category | flops | bytes accessed | tf_op | source)
XLA Modules:
  0.0 165.0 jit_solution(17145491766048197165)
XLA Ops:
  0.6 1.5 collective-permute-start
  2.1 1.4 copy.15.pattern
  3.5 0.7 pad_add_fusion.ids
  4.1 6.2 %shard_map.138 = (f32[512,1024]{1,0:T(8,128)}, f32[512,1024]{1,0:T(8,128)}, f32[544,256]{1,0:T(8,128)}) custom-call(s32[2]{0:T(128)} %pad_add_fusion.ids, s32[16,4]{1,0:T(8,128)} %copy.15.pattern, f32[1024,1536]{1,0:T(8,128)} %panel.2, f32[1024,1536]{1,0:T(8,128)} %panel.2, f32[1536,256]{1,0:T(8,128)} %diag.2), custom_call_target="tpu_custom_call" | custom-call | flops 1024 | bytes 1024 | tf_op jit(solution)/shard_map/pallas_call | solution.py:121
  10.9 1.5 collective-permute-start.2
  12.4 6.1 %shard_map.136 = (f32[512,1024]{1,0:T(8,128)}, f32[512,1024]{1,0:T(8,128)}, f32[544,256]{1,0:T(8,128)}) custom-call(s32[2]{0:T(128)} %pad_add_fusion.ids, s32[16,4]{1,0:T(8,128)} %copy.15.pattern, f32[1024,1536]{1,0:T(8,128)} %panel.2, f32[1024,1536]{1,0:T(8,128)} %panel.2, f32[1536,256]{1,0:T(8,128)} %diag.2), custom_call_target="tpu_custom_call" | custom-call | flops 1024 | bytes 1024 | tf_op jit(solution)/shard_map/pallas_call | solution.py:121
  18.5 0.7 copy.16.pattern
  19.2 0.9 copy-done.14
  20.1 7.9 %shard_map.137 = (f32[1160,256]{1,0:T(8,128)}, f32[1160,256]{1,0:T(8,128)}, f32[576,256]{1,0:T(8,128)}, f32[584,256]{1,0:T(8,128)}, f32[576,256]{1,0:T(8,128)}, /*index=5*/f32[584,256]{1,0:T(8,128)}) custom-call(s32[2]{0:T(128)} %pad_add_fusion.ids, s32[32,4]{1,0:T(8,128)} %copy.16.pattern, f32[1024,768]{1,0:T(8,128)} %panel.3, ...), custom_call_target="tpu_custom_call" | custom-call | flops 1024 | bytes 1024 | tf_op jit(solution)/shard_map/pallas_call | solution.py:166
  28.0 1.4 collective-permute-start.3
  29.4 1.3 collective-permute-start.4
  31.4 2.1 %add.36 = f32[512,1024]{1,0:T(8,128)S(1)} add(f32[512,1024]{1,0:T(8,128)S(1)} %copy-done.8, f32[512,1024]{1,0:T(8,128)} %collective-permute-done.5) | non-fusion elementwise | flops 524288 | bytes 6291456 | tf_op jit(solution)/shard_map/add | solution.py:382
  33.6 0.9 collective-permute-done.6.own_core
  35.4 0.8 copy-done.21
  36.2 5.3 %shard_map.139 = (bf16[1024,1024]{1,0:T(8,128)(2,1)}, bf16[1024,1024]{1,0:T(8,128)(2,1)}) custom-call(s32[2]{0:T(128)} %pad_add_fusion.ids, f32[256,1024]{1,0:T(8,128)} %own.1, f32[256,1024]{1,0:T(8,128)} %copy-done.13, f32[256,512]{1,0:T(8,128)} %collective-permute-done.2.far, f32[256,512]{1,0:T(8,128)} %copy-done.21), custom_call_target="tpu_custom_call" | custom-call | flops 1024 | bytes 1024 | tf_op jit(solution)/shard_map/pallas_call | solution.py:188
  41.5 15.4 %shard_map.140 = (f32[256,1536]{1,0:T(8,128)}, f32[384,256]{1,0:T(8,128)}) custom-call(s32[2]{0:T(128)} %pad_add_fusion.ids, bf16[1024,1024]{1,0:T(8,128)(2,1)} %get-tuple-element.82.hi, bf16[1024,1024]{1,0:T(8,128)(2,1)} %get-tuple-element.63.lo, f32[1024,1536]{1,0:T(8,128)} %panel.2, f32[1536,256]{1,0:T(8,128)} %diag.2), custom_call_target="tpu_custom_call" | custom-call | flops 1024 | bytes 1024 | tf_op jit(solution)/shard_map/pallas_call | solution.py:230
  57.2 1.0 collective-permute-start.14
  58.3 1.1 collective-permute-start.8
  59.5 1.7 %collective-permute-start.9 = (f32[584,256]{1,0:T(8,128)S(1)}, f32[584,256]{1,0:T(8,128)S(1)}, u32[]{:S(2)}, u32[]{:S(2)}) collective-permute-start(f32[584,256]{1,0:T(8,128)S(1)} %slice_add_fusion), channel_id=1, source_target_pairs={{0,3},{1,0},{2,1},{3,2},{4,7},{5,4},{6,5},{7,6},{8,11},{9,8},{10,9... | collective-permute-start | bytes 1794056 | tf_op jit(solution)/shard_map/ppermute | solution.py:21
  61.2 13.3 %collective-permute-done.8 = f32[576,256]{1,0:T(8,128)S(1)} collective-permute-done((f32[576,256]{1,0:T(8,128)S(1)}, f32[576,256]{1,0:T(8,128)S(1)}, u32[]{:S(2)}, u32[]{:S(2)}) %collective-permute-start.8) | collective-permute-done | bytes 589856 | tf_op jit(solution)/shard_map/ppermute | solution.py:21
  74.9 2.6 %collective-permute-start.11 = (f32[584,256]{1,0:T(8,128)S(1)}, f32[584,256]{1,0:T(8,128)S(1)}, u32[]{:S(2)}, u32[]{:S(2)}) collective-permute-start(f32[584,256]{1,0:T(8,128)S(1)} %add_add_fusion.1.refs_1_), channel_id=1, source_target_pairs={{0,3},{1,0},{2,1},{3,2},{4,7},{5,4},{6,5},{7,6},{8,11},{9,8},{10,9... | collective-permute-start | bytes 1794056 | tf_op jit(solution)/shard_map/ppermute | solution.py:21
  77.6 15.6 %collective-permute-done.13 = f32[544,256]{1,0:T(8,128)S(1)} collective-permute-done((f32[544,256]{1,0:T(8,128)S(1)}, f32[544,256]{1,0:T(8,128)S(1)}, u32[]{:S(2)}, u32[]{:S(2)}) %collective-permute-start.13) | collective-permute-done | bytes 557088 | tf_op jit(solution)/shard_map/ppermute | solution.py:26
  93.3 0.7 add_add_fusion.own
  94.0 1.3 collective-permute-start.15
  96.2 2.3 %collective-permute-start.18 = (f32[1160,256]{1,0:T(8,128)S(1)}, f32[1160,256]{1,0:T(8,128)S(1)}, u32[]{:S(2)}, u32[]{:S(2)}) collective-permute-start(f32[1160,256]{1,0:T(8,128)S(1)} %get-tuple-element.93), channel_id=1, source_target_pairs={{0,3},{1,0},{2,1},{3,2},{4,7},{5,4},{6,5},{7,6},{8,11},{9,8},{10,9... | collective-permute-start | bytes 3563528 | tf_op jit(solution)/shard_map/ppermute | solution.py:21
  98.6 1.4 collective-permute-start.16
  100.0 1.6 collective-permute-done.16.d1
  101.6 0.8 copy-done.20
  102.4 1.3 copy-done.10
  103.7 27.5 %shard_map.141 = (f32[1024,768]{1,0:T(8,128)}, f32[768,256]{1,0:T(8,128)}, bf16[1024,1024]{1,0:T(8,128)(2,1)}, bf16[1024,1024]{1,0:T(8,128)(2,1)}) custom-call(s32[2]{0:T(128)} %pad_add_fusion.ids, bf16[1024,1024]{1,0:T(8,128)(2,1)} %get-tuple-element.82.hi, bf16[1024,1024]{1,0:T(8,128)(2,1)} %get-tuple-element.63.lo, f32[512,1024]{1,0:T(8,128)} %copy-done, ...), custom_call_target="tpu_custom_call" | custom-call | flops 1024 | bytes 1024 | tf_op jit(solution)/shard_map/pallas_call | solution.py:306
  131.2 1.0 copy-done.11
  132.7 32.3 %shard_map.142 = (f32[1024,1536]{1,0:T(8,128)}, f32[1536,256]{1,0:T(8,128)}) custom-call(s32[2]{0:T(128)} %pad_add_fusion.ids, bf16[1024,1024]{1,0:T(8,128)(2,1)} %get-tuple-element.90.hi, bf16[1024,1024]{1,0:T(8,128)(2,1)} %get-tuple-element.91.lo, f32[576,256]{1,0:T(8,128)} %copy-done.2, f32[584,256]{1,0:T(8,128)} %copy-done.1, f32[576,256]{1,0:T(8,128)} %copy-done.6, ...), custom_call_target="tpu_custom_call" | custom-call | flops 1024 | bytes 1024 | tf_op jit(solution)/shard_map/pallas_call | solution.py:345
  (73 shorter events, 4.7 us)
Async XLA Ops:
  0.6 18.6 %collective-permute-start = (f32[1024,768]{1,0:T(8,128)}, f32[1024,768]{1,0:T(8,128)}, u32[]{:S(2)}, u32[]{:S(2)}) collective-permute-start(f32[1024,768]{1,0:T(8,128)} %panel.3), channel_id=1, source_target_pairs={{0,4},{4,0},{8,12},{12,8},{16,20},{20,16},{24,28},{28,24},{32,36},... | collective-permute-start | bytes 9437192 | tf_op jit(solution)/shard_map/ppermute | solution.py:26
  4.1 6.2 %copy-start.4 = (f32[768,256]{1,0:T(8,128)S(1)}, f32[768,256]{1,0:T(8,128)}, u32[]{:S(2)}) copy-start(f32[768,256]{1,0:T(8,128)} %diag.3) | copy-start | bytes 2359300
  4.1 6.7 %copy-start.3 = (f32[256,1024]{1,0:T(8,128)S(1)}, f32[256,1024]{1,0:T(8,128)}, u32[]{:S(2)}) copy-start(f32[256,1024]{1,0:T(8,128)} %own.1) | copy-start | bytes 3145732
  10.3 21.1 %collective-permute-start.5 = (f32[512,1024]{1,0:T(8,128)}, f32[512,1024]{1,0:T(8,128)}, u32[]{:S(2)}, u32[]{:S(2)}) collective-permute-start(f32[512,1024]{1,0:T(8,128)} %get-tuple-element.58), channel_id=1, source_target_pairs={{0,4},{4,0},{8,12},{12,8},{16,20},{20,16},{24,28},{28,24},{32,36},... | collective-permute-start | bytes 6291464 | tf_op jit(solution)/shard_map/ppermute | solution.py:26
  10.3 8.9 %collective-permute-start.1 = (f32[768,256]{1,0:T(8,128)S(1)}, f32[768,256]{1,0:T(8,128)S(1)}, u32[]{:S(2)}, u32[]{:S(2)}) collective-permute-start(f32[768,256]{1,0:T(8,128)S(1)} %copy-done.4), channel_id=1, source_target_pairs={{0,4},{4,0},{8,12},{12,8},{16,20},{20,16},{24,28},{28,24},{32,36},... | collective-permute-start | bytes 2359304 | tf_op jit(solution)/shard_map/ppermute | solution.py:26
  10.9 7.6 %copy-start.22 = (s32[32,4]{0,1:T(4,128)S(1)}, s32[32,4]{0,1:T(4,128)}, u32[]{:S(2)}) copy-start(s32[32,4]{0,1:T(4,128)} %param.17) | copy-start | bytes 1540
  10.9 17.1 %collective-permute-start.2 = (f32[256,512]{1,0:T(8,128)S(1)}, f32[256,512]{1,0:T(8,128)}, u32[]{:S(2)}, u32[]{:S(2)}) collective-permute-start(f32[256,512]{1,0:T(8,128)S(1)} %slice_select_fusion), channel_id=1, source_target_pairs={{0,8},{4,12},{8,0},{12,4},{16,24},{20,28},{24,16},{28,20},{32,40},... | collective-permute-start | bytes 1572872 | tf_op jit(solution)/shard_map/ppermute | solution.py:26
  19.2 12.2 %copy-start.8 = (f32[512,1024]{1,0:T(8,128)S(1)}, f32[512,1024]{1,0:T(8,128)}, u32[]{:S(2)}) copy-start(f32[512,1024]{1,0:T(8,128)} %get-tuple-element.57) | copy-start | bytes 6291460
  28.0 29.2 %collective-permute-start.3 = (f32[1160,256]{1,0:T(8,128)}, f32[1160,256]{1,0:T(8,128)S(1)}, u32[]{:S(2)}, u32[]{:S(2)}) collective-permute-start(f32[1160,256]{1,0:T(8,128)} %get-tuple-element.55), channel_id=1, source_target_pairs={{0,1},{1,2},{2,3},{3,0},{4,5},{5,6},{6,7},{7,4},{8,9},{9,10},{10,1... | collective-permute-start | bytes 3563528 | tf_op jit(solution)/shard_map/ppermute | solution.py:21
  29.4 27.8 %collective-permute-start.4 = (f32[1160,256]{1,0:T(8,128)}, f32[1160,256]{1,0:T(8,128)S(1)}, u32[]{:S(2)}, u32[]{:S(2)}) collective-permute-start(f32[1160,256]{1,0:T(8,128)} %get-tuple-element.56), channel_id=1, source_target_pairs={{0,3},{1,0},{2,1},{3,2},{4,7},{5,4},{6,5},{7,6},{8,11},{9,8},{10,9... | collective-permute-start | bytes 3563528 | tf_op jit(solution)/shard_map/ppermute | solution.py:21
  30.8 3.7 %collective-permute-start.6 = (f32[256,1024]{1,0:T(8,128)S(1)}, f32[256,1024]{1,0:T(8,128)S(1)}, u32[]{:S(2)}, u32[]{:S(2)}) collective-permute-start(f32[256,1024]{1,0:T(8,128)S(1)} %copy-done.3), channel_id=1, source_target_pairs={{0,4},{4,0},{8,12},{12,8},{16,20},{20,16},{24,28},{28,24},{32,36},... | collective-permute-start | bytes 3145736 | tf_op jit(solution)/shard_map/ppermute | solution.py:26
  31.4 4.0 %collective-permute-start.7 = (f32[256,512]{1,0:T(8,128)}, f32[256,512]{1,0:T(8,128)S(1)}, u32[]{:S(2)}, u32[]{:S(2)}) collective-permute-start(f32[256,512]{1,0:T(8,128)} %collective-permute-done.2.far), channel_id=1, source_target_pairs={{0,4},{4,0},{8,12},{12,8},{16,20},{20,16},{24,28},{28,24},{32,36},... | collective-permute-start | bytes 1572872 | tf_op jit(solution)/shard_map/ppermute | solution.py:26
  34.5 58.8 %collective-permute-start.12 = (f32[512,1024]{1,0:T(8,128)S(1)}, f32[512,1024]{1,0:T(8,128)S(1)}, u32[]{:S(2)}, u32[]{:S(2)}) collective-permute-start(f32[512,1024]{1,0:T(8,128)S(1)} %add.36), channel_id=1, source_target_pairs={{0,8},{4,12},{8,0},{12,4},{16,24},{20,28},{24,16},{28,20},{32,40},... | collective-permute-start | bytes 6291464 | tf_op jit(solution)/shard_map/ppermute | solution.py:26
  41.5 16.7 %copy-start.17 = (f32[576,256]{1,0:T(8,128)S(1)}, f32[576,256]{1,0:T(8,128)}, u32[]{:S(2)}) copy-start(f32[576,256]{1,0:T(8,128)} %get-tuple-element.71) | copy-start | bytes 1769476
  56.9 17.7 %copy-start.18 = (f32[576,256]{1,0:T(8,128)S(1)}, f32[576,256]{1,0:T(8,128)}, u32[]{:S(2)}) copy-start(f32[576,256]{1,0:T(8,128)} %get-tuple-element.69) | copy-start | bytes 1769476
  57.2 36.1 %collective-permute-start.14 = (f32[512,1024]{1,0:T(8,128)}, f32[512,1024]{1,0:T(8,128)S(1)}, u32[]{:S(2)}, u32[]{:S(2)}) collective-permute-start(f32[512,1024]{1,0:T(8,128)} %get-tuple-element.84), channel_id=1, source_target_pairs={{0,4},{4,0},{8,12},{12,8},{16,20},{20,16},{24,28},{28,24},{32,36},... | collective-permute-start | bytes 6291464 | tf_op jit(solution)/shard_map/ppermute | solution.py:26
  58.3 16.5 %copy-start.16 = (f32[584,256]{1,0:T(8,128)S(1)}, f32[584,256]{1,0:T(8,128)}, u32[]{:S(2)}) copy-start(f32[584,256]{1,0:T(8,128)} %get-tuple-element.73) | copy-start | bytes 1794052
  58.3 16.2 %collective-permute-start.8 = (f32[576,256]{1,0:T(8,128)S(1)}, f32[576,256]{1,0:T(8,128)S(1)}, u32[]{:S(2)}, u32[]{:S(2)}) collective-permute-start(f32[576,256]{1,0:T(8,128)S(1)} %slice_add_fusion.1), channel_id=1, source_target_pairs={{0,1},{1,2},{2,3},{3,0},{4,5},{5,6},{6,7},{7,4},{8,9},{9,10},{10,1... | collective-permute-start | bytes 1769480 | tf_op jit(solution)/shard_map/ppermute | solution.py:21
  59.5 15.2 %collective-permute-start.9 = (f32[584,256]{1,0:T(8,128)S(1)}, f32[584,256]{1,0:T(8,128)S(1)}, u32[]{:S(2)}, u32[]{:S(2)}) collective-permute-start(f32[584,256]{1,0:T(8,128)S(1)} %slice_add_fusion), channel_id=1, source_target_pairs={{0,3},{1,0},{2,1},{3,2},{4,7},{5,4},{6,5},{7,6},{8,11},{9,8},{10,9... | collective-permute-start | bytes 1794056 | tf_op jit(solution)/shard_map/ppermute | solution.py:21
  74.5 2.9 %copy-start.23 = (f32[544,256]{1,0:T(8,128)S(1)}, f32[544,256]{1,0:T(8,128)}, u32[]{:S(2)}) copy-start(f32[544,256]{1,0:T(8,128)} %get-tuple-element.79) | copy-start | bytes 1671172
  74.5 18.7 %copy-start.9 = (f32[512,1024]{1,0:T(8,128)S(1)}, f32[512,1024]{1,0:T(8,128)}, u32[]{:S(2)}) copy-start(f32[512,1024]{1,0:T(8,128)} %get-tuple-element.83) | copy-start | bytes 6291460
  74.7 20.6 %copy-start.2 = (f32[576,256]{1,0:T(8,128)}, f32[576,256]{1,0:T(8,128)S(1)}, u32[]{:S(2)}) copy-start(f32[576,256]{1,0:T(8,128)S(1)} %add_add_fusion.2.refs_0_) | copy-start | bytes 1769476
  74.9 20.4 %copy-start.1 = (f32[584,256]{1,0:T(8,128)}, f32[584,256]{1,0:T(8,128)S(1)}, u32[]{:S(2)}) copy-start(f32[584,256]{1,0:T(8,128)S(1)} %add_add_fusion.1.refs_1_) | copy-start | bytes 1794052
  74.9 18.4 %collective-permute-start.11 = (f32[584,256]{1,0:T(8,128)S(1)}, f32[584,256]{1,0:T(8,128)S(1)}, u32[]{:S(2)}, u32[]{:S(2)}) collective-permute-start(f32[584,256]{1,0:T(8,128)S(1)} %add_add_fusion.1.refs_1_), channel_id=1, source_target_pairs={{0,3},{1,0},{2,1},{3,2},{4,7},{5,4},{6,5},{7,6},{8,11},{9,8},{10,9... | collective-permute-start | bytes 1794056 | tf_op jit(solution)/shard_map/ppermute | solution.py:21
  77.5 15.8 %collective-permute-start.10 = (f32[576,256]{1,0:T(8,128)S(1)}, f32[576,256]{1,0:T(8,128)S(1)}, u32[]{:S(2)}, u32[]{:S(2)}) collective-permute-start(f32[576,256]{1,0:T(8,128)S(1)} %add_add_fusion.2.refs_0_), channel_id=1, source_target_pairs={{0,1},{1,2},{2,3},{3,0},{4,5},{5,6},{6,7},{7,4},{8,9},{9,10},{10,1... | collective-permute-start | bytes 1769480 | tf_op jit(solution)/shard_map/ppermute | solution.py:21
  77.5 15.8 %collective-permute-start.13 = (f32[544,256]{1,0:T(8,128)S(1)}, f32[544,256]{1,0:T(8,128)S(1)}, u32[]{:S(2)}, u32[]{:S(2)}) collective-permute-start(f32[544,256]{1,0:T(8,128)S(1)} %copy-done.23), channel_id=1, source_target_pairs={{0,8},{4,12},{8,0},{12,4},{16,24},{20,28},{24,16},{28,20},{32,40},... | collective-permute-start | bytes 1671176 | tf_op jit(solution)/shard_map/ppermute | solution.py:26
  94.0 4.5 %copy-start.19 = (f32[544,256]{1,0:T(8,128)S(1)}, f32[544,256]{1,0:T(8,128)}, u32[]{:S(2)}) copy-start(f32[544,256]{1,0:T(8,128)} %get-tuple-element.86) | copy-start | bytes 1671172
  94.0 7.6 %collective-permute-start.15 = (f32[512,1024]{1,0:T(8,128)S(1)}, f32[512,1024]{1,0:T(8,128)S(1)}, u32[]{:S(2)}, u32[]{:S(2)}) collective-permute-start(f32[512,1024]{1,0:T(8,128)S(1)} %add_add_fusion.own), channel_id=1, source_target_pairs={{0,4},{4,0},{8,12},{12,8},{16,20},{20,16},{24,28},{28,24},{32,36},... | collective-permute-start | bytes 6291464 | tf_op jit(solution)/shard_map/ppermute | solution.py:26
  95.5 35.6 %collective-permute-start.17 = (f32[1160,256]{1,0:T(8,128)S(1)}, f32[1160,256]{1,0:T(8,128)S(1)}, u32[]{:S(2)}, u32[]{:S(2)}) collective-permute-start(f32[1160,256]{1,0:T(8,128)S(1)} %get-tuple-element.92), channel_id=1, source_target_pairs={{0,1},{1,2},{2,3},{3,0},{4,5},{5,6},{6,7},{7,4},{8,9},{9,10},{10,1... | collective-permute-start | bytes 3563528 | tf_op jit(solution)/shard_map/ppermute | solution.py:21
  96.2 35.0 %collective-permute-start.18 = (f32[1160,256]{1,0:T(8,128)S(1)}, f32[1160,256]{1,0:T(8,128)S(1)}, u32[]{:S(2)}, u32[]{:S(2)}) collective-permute-start(f32[1160,256]{1,0:T(8,128)S(1)} %get-tuple-element.93), channel_id=1, source_target_pairs={{0,3},{1,0},{2,1},{3,2},{4,7},{5,4},{6,5},{7,6},{8,11},{9,8},{10,9... | collective-permute-start | bytes 3563528 | tf_op jit(solution)/shard_map/ppermute | solution.py:21
  98.5 3.0 %copy-start.7 = (f32[544,256]{1,0:T(8,128)}, f32[544,256]{1,0:T(8,128)S(1)}, u32[]{:S(2)}) copy-start(f32[544,256]{1,0:T(8,128)S(1)} %add.45.d0) | copy-start | bytes 1671172
  98.6 3.0 %collective-permute-start.16 = (f32[544,256]{1,0:T(8,128)S(1)}, f32[544,256]{1,0:T(8,128)S(1)}, u32[]{:S(2)}, u32[]{:S(2)}) collective-permute-start(f32[544,256]{1,0:T(8,128)S(1)} %add.45.d0), channel_id=1, source_target_pairs={{0,4},{4,0},{8,12},{12,8},{16,20},{20,16},{24,28},{28,24},{32,36},... | collective-permute-start | bytes 1671176 | tf_op jit(solution)/shard_map/ppermute | solution.py:26
  (11 other events, 15.5 us)
